TPU v7x, 512 devices: a whole 4x4x16 slice. The times are simulated.
512 devices in a mesh: row: 8 (over x_lo, y), col: 64 (over z, x_hi, core).
Axes of the slice: x: 4 (x_hi: 2, x_lo: 2; x = x_hi * 2 + x_lo), y: 4, z: 16, core: 2. Of those that a mesh axis runs over, the one named last changes fastest.
Arguments:
- tiles: bfloat16 [512, 384, 512], P('row', 'col')
- block_cols: int32 [8, 384], P('row', 'col'), may hold values from 0 to 7, as said below
- signs: int32 [262144], P('col'), may hold values from -1 to 1, as said below
- samples: int32 [4096], replicated, may hold values from 0 to 262143, as said below
Outputs:
- sketch: float32 [512, 4096], P('row', 'col')
- gram: float32 [4096, 4096], P('row', 'col')
Inputs may be any that keep to these rules, and one draw needn't show every extreme that they name: `signs`: every entry is -1 or +1. The 6 entries block_cols[r, c * 6 + t], t < 6, of one row slab r and column slab c are distinct. `samples`: entry k lies in column slab k // 64, that is from (k // 64) * 4096 to (k // 64 + 1) * 4096 - 1; the 64 entries of one slab are distinct.
All inputs are finite; a program needn't handle non-finite values.
Results may differ from a plain program's by a relative error of at most 0.004.
Values may be sent and summed in bfloat16 or wider, within the bound.
A program may use at most 64 MiB of HBM per device.

v0:
```python
import functools
import math

import jax
import jax.numpy as jnp
from jax import lax
from jax.experimental import pallas as pl
from jax.experimental.pallas import tpu as pltpu
from jax.sharding import PartitionSpec as P

MESH = pl.DeviceIdType.MESH
CHIPS = 2
CORES = 2
QUAD = CHIPS * CORES
LANES = 128
F32 = jnp.float32
BF16 = jnp.bfloat16


def parity_sign(bits):
    for shift in (8, 4, 2, 1):
        bits = bits ^ (bits >> shift)
    return (1 - 2 * (bits & 1)).astype(F32)


def alternating(k):
    return lax.div(k + 1, 2) * (1 - 2 * lax.rem(k, 2))


def remote(src, dst, send_sem, recv_sem, device):
    return pltpu.make_async_remote_copy(
        src_ref=src,
        dst_ref=dst,
        send_sem=send_sem,
        recv_sem=recv_sem,
        device_id=device,
        device_id_type=MESH,
    )


def wait_bytes(ref, sem):
    pltpu.make_async_copy(ref, ref, sem).wait()


def kernel(
    nrow,
    nz,
    tiles_hbm,
    block_hbm,
    signs_hbm,
    samples_hbm,
    sketch_ref,
    gram_ref,
    tl,
    blocks,
    signs,
    samples,
    xs,
    hop,
    terms,
    terms2,
    halves,
    other,
    other2,
    own,
    csend,
    crecv,
    ag,
    sk,
    sc,
    sr,
    gs,
    gr,
    in_sem,
    a_send,
    a_recv,
    x_send,
    x_recv,
    c_send,
    c_recv,
    g_send,
    g_recv,
    k_send,
    k_recv,
    s_send,
    s_recv,
    f_send,
    f_recv,
    o_send,
    o_recv,
):
    slots, rows, tile_width = tl.shape
    part = rows // CORES
    width = samples.shape[0] * LANES
    planes = nz // nrow
    chunk = planes * CHIPS * LANES
    nchunk = width // chunk
    row = lax.axis_index("row")
    col = lax.axis_index("col")
    z = lax.div(col, QUAD)
    q = lax.rem(col, QUAD)
    h = lax.div(q, CORES)
    core = lax.rem(q, CORES)
    my_chunk = lax.div(z, planes)
    sibling = (row, col + 1 - 2 * core)
    partner = (row, col + CORES * (1 - 2 * h))

    def at(z2, h2, core2):
        return z2 * QUAD + h2 * CORES + core2

    def far_first(k):
        return nz // 2 + alternating(k)

    fetches = [
        pltpu.make_async_copy(src, dst, in_sem.at[i])
        for i, (src, dst) in enumerate(
            [(block_hbm, blocks), (signs_hbm, signs), (tiles_hbm, tl), (samples_hbm, samples)]
        )
    ]
    for fetch in fetches:
        fetch.start()

    barrier = pltpu.get_barrier_semaphore()

    def greet_plane(k, _):
        mate = lax.rem(row * QUAD + q + k, nrow * QUAD)
        device = (lax.div(mate, QUAD), z * QUAD + lax.rem(mate, QUAD))
        pl.semaphore_signal(barrier, inc=1, device_id=device, device_id_type=MESH)
        return 0

    def greet_line(k, _):
        device = (row, at(lax.rem(z + far_first(k), nz), h, core))
        pl.semaphore_signal(barrier, inc=1, device_id=device, device_id_type=MESH)
        return 0

    lax.fori_loop(0, nz - 1, greet_line, 0)
    lax.fori_loop(1, nrow * QUAD, greet_plane, 0)

    per_block = tile_width // LANES
    where_row = lax.broadcasted_iota(jnp.int32, (8, LANES), 0)
    codes = jnp.zeros((8, LANES), jnp.int32)
    for fetch in fetches[:3]:
        fetch.wait()
    for t in range(slots):
        block = blocks[0, t]
        codes = jnp.where(where_row == t, col * (signs.shape[0] // per_block) + block, codes)
        for j in range(per_block):
            sign = signs[pl.ds(block * per_block + j, 1), :].astype(F32)
            sign = jnp.broadcast_to(sign, (rows, LANES)).astype(BF16)
            cut = slice(j * LANES, (j + 1) * LANES)
            xs[t * rows : (t + 1) * rows, cut] = tl[t, :, cut] * sign

    low_bits = (tile_width - 1).bit_length()
    fetches[3].wait()

    def fill(blk, _):
        low = samples[pl.ds(blk, 1), :] & (tile_width - 1)
        lanes = pl.ds(pl.multiple_of(blk * LANES, LANES), LANES)
        base = parity_sign(lax.broadcasted_iota(jnp.int32, (16, LANES), 0) & low).astype(BF16)
        group = [base]
        for bit in range(4, low_bits):
            sign = (1 - 2 * ((low >> bit) & 1)).astype(F32)
            sign = jnp.broadcast_to(sign, (16, LANES)).astype(BF16)
            group = group + [g * sign for g in group]
        for i, g in enumerate(group):
            hop[16 * i : 16 * i + 16, lanes] = g
        return 0

    lax.fori_loop(0, width // LANES, fill, 0)

    def chunk_of(k):
        return lax.rem(my_chunk + nchunk // 2 + alternating(k) + nchunk, nchunk)

    def multiply(k, _):
        ch = chunk_of(k)
        operator = hop[:, pl.ds(pl.multiple_of(ch * chunk, chunk), chunk)]
        y = jnp.dot(xs[...], operator, preferred_element_type=F32)
        for i in range(chunk // LANES):
            high = samples[pl.ds(ch * (chunk // LANES) + i, 1), :] >> low_bits
            coef = parity_sign(codes & high)
            total = None
            for t in range(slots):
                term = y[t * rows : (t + 1) * rows, i * LANES : (i + 1) * LANES] * coef[t : t + 1, :]
                total = term if total is None else total + term
            for p in range(CORES):
                terms[k, p, :, i * LANES : (i + 1) * LANES] = total[p * part : (p + 1) * part]
        return 0

    lax.fori_loop(0, nchunk, multiply, 0)

    pl.semaphore_wait(barrier, nz - 1 + nrow * QUAD - 1)

    def to_sibling(k, _):
        remote(terms.at[k, 1 - core], terms2.at[k], a_send, a_recv.at[k], sibling).start()
        return 0

    lax.fori_loop(0, nchunk, to_sibling, 0)

    def to_partner(k, _):
        wait_bytes(terms2.at[k], a_recv.at[k])
        total = terms[k, core] + terms2[k]
        for i in range(planes):
            left = total[:, 2 * i * LANES : (2 * i + 1) * LANES]
            right = total[:, (2 * i + 1) * LANES : (2 * i + 2) * LANES]
            halves[k, i] = jnp.where(h == 0, left, right)
            other[k, i] = jnp.where(h == 0, right, left)
        remote(other.at[k], other2.at[k], x_send, x_recv.at[k], partner).start()
        return 0

    lax.fori_loop(0, nchunk, to_partner, 0)

    def to_planes(k, _):
        wait_bytes(other2.at[k], x_recv.at[k])
        for i in range(planes):
            z2 = chunk_of(k) * planes + i
            total = halves[k, i] + other2[k, i]

            @pl.when(z2 == z)
            def _():
                own[...] = total

            @pl.when(z2 != z)
            def _():
                csend[z2] = total.astype(BF16)
                slot = lax.rem(z - z2 + nz, nz) - 1
                remote(csend.at[z2], crecv.at[slot], c_send, c_recv, (row, at(z2, h, core))).start()

        return 0

    lax.fori_loop(0, nchunk, to_planes, 0)

    wait_bytes(crecv, c_recv)
    total = own[...]
    for i in range(nz - 1):
        total = total + crecv[i].astype(F32)
    total = total * (1.0 / math.sqrt(width))
    ag[z] = total.astype(BF16)

    def spread(k, _):
        device = (row, at(lax.rem(z + far_first(k), nz), h, core))
        remote(ag.at[z], ag.at[z], g_send, g_recv.at[z], device).start()
        return 0

    lax.fori_loop(0, nz - 1, spread, 0)

    my_rows = pl.ds(pl.multiple_of(row * rows + core * part, part), part)

    def in_plane(k, _):
        mate = lax.rem(row * CORES + core + k, nrow * CORES)
        device = (lax.div(mate, CORES), at(z, h, lax.rem(mate, CORES)))
        remote(ag.at[z], sc.at[my_rows], s_send, s_recv, device).start()
        return 0

    lax.fori_loop(1, nrow * CORES, in_plane, 0)
    pltpu.make_async_copy(ag.at[z], sc.at[my_rows], s_recv).start()

    sk[0] = total
    swap_sketch = remote(sk.at[0], sk.at[1], k_send, k_recv, sibling)
    swap_sketch.start()

    my_cols = pl.ds(pl.multiple_of(h * LANES, LANES), LANES)

    def forward(k, _):
        p = lax.rem(my_chunk + alternating(k) + nrow, nrow)
        for i in range(planes):
            z2 = p * planes + i

            @pl.when(z2 != z)
            def _():
                wait_bytes(ag.at[z2], g_recv.at[z2])

            for h2 in range(CHIPS):
                here = jnp.logical_and(p == row, jnp.logical_and(h2 == h, i == core))

                @pl.when(here)
                def _():
                    pltpu.make_async_copy(ag.at[z2], sr.at[my_rows, my_cols], f_recv).start()

                @pl.when(jnp.logical_not(here))
                def _():
                    remote(
                        ag.at[z2], sr.at[my_rows, my_cols], f_send, f_recv, (p, at(z, h2, i))
                    ).start()

        return 0

    lax.fori_loop(0, nrow, forward, 0)

    half = LANES // CORES
    swap_sketch.wait()
    for i in range(CORES):
        block = sk[jnp.where(core == i, 0, 1)]
        sketch_ref[i * part : (i + 1) * part, :] = jnp.where(core == 0, block[:, :half], block[:, half:])

    wait_bytes(sc, s_recv)
    wait_bytes(sr, f_recv)
    product = lax.dot_general(
        sc[...], sr[...], (((0,), (0,)), ((), ())), preferred_element_type=F32
    ) * (1.0 / (rows * nrow))
    gs[...] = jnp.where(core == 0, product[half:], product[:half])
    swap_product = remote(gs, gr, o_send, o_recv, sibling)
    swap_product.start()
    mine = jnp.where(core == 0, product[:half], product[half:])
    swap_product.wait()
    theirs = gr[...]
    cols = CHIPS * LANES
    gram_ref[:, :cols] = jnp.where(core == 0, mine, theirs)
    gram_ref[:, cols:] = jnp.where(core == 0, theirs, mine)

    wait_bytes(terms2, a_send)
    wait_bytes(other2, x_send)
    wait_bytes(crecv, c_send)
    wait_bytes(crecv, g_send)
    wait_bytes(sc.at[pl.ds(0, rows * nrow - part)], s_send)
    wait_bytes(sr.at[pl.ds(0, rows * nrow - part // CHIPS)], f_send)


def per_device(nrow, nz, tiles, block_cols, signs, samples):
    rows, slots, tile_width = tiles.shape
    width = samples.shape[0]
    part = rows // CORES
    half = LANES // CORES
    planes = nz // nrow
    chunk = planes * CHIPS * LANES
    nchunk = width // chunk
    dma = pltpu.SemaphoreType.DMA
    vmem = pl.BlockSpec(memory_space=pltpu.VMEM)
    hbm = pl.BlockSpec(memory_space=pltpu.HBM)
    sketch, gram_t = pl.pallas_call(
        functools.partial(kernel, nrow, nz),
        out_shape=(
            jax.ShapeDtypeStruct((rows, half), F32),
            jax.ShapeDtypeStruct((half, width // nrow), F32),
        ),
        in_specs=[hbm, hbm, hbm, hbm],
        out_specs=(vmem, vmem),
        scratch_shapes=[
            pltpu.VMEM((slots, rows, tile_width), BF16),
            pltpu.SMEM(block_cols.shape, jnp.int32),
            pltpu.VMEM((signs.shape[0] // LANES, LANES), jnp.int32),
            pltpu.VMEM((width // LANES, LANES), jnp.int32),
            pltpu.VMEM((slots * rows, tile_width), BF16),
            pltpu.VMEM((tile_width, width), BF16),
            pltpu.VMEM((nchunk, CORES, part, chunk), F32),
            pltpu.VMEM((nchunk, part, chunk), F32),
            pltpu.VMEM((nchunk, planes, part, LANES), F32),
            pltpu.VMEM((nchunk, planes, part, LANES), F32),
            pltpu.VMEM((nchunk, planes, part, LANES), F32),
            pltpu.VMEM((part, LANES), F32),
            pltpu.VMEM((nz, part, LANES), BF16),
            pltpu.VMEM((nz - 1, part, LANES), BF16),
            pltpu.VMEM((nz, part, LANES), BF16),
            pltpu.VMEM((2, part, LANES), F32),
            pltpu.VMEM((rows * nrow, LANES), BF16),
            pltpu.VMEM((rows * nrow, CHIPS * LANES), BF16),
            pltpu.VMEM((half, CHIPS * LANES), F32),
            pltpu.VMEM((half, CHIPS * LANES), F32),
            dma((4,)),
            dma,
            dma((nchunk,)),
            dma,
            dma((nchunk,)),
            dma,
            dma,
            dma,
            dma((nz,)),
            dma,
            dma,
            dma,
            dma,
            dma,
            dma,
            dma,
            dma,
        ],
        compiler_params=pltpu.CompilerParams(
            collective_id=0, has_side_effects=True, vmem_limit_bytes=32 << 20
        ),
    )(
        *(
            pltpu.with_memory_space_constraint(x, pltpu.HBM)
            for x in (
                tiles.transpose(1, 0, 2),
                block_cols,
                signs.reshape(-1, LANES),
                samples.reshape(-1, LANES),
            )
        )
    )
    return sketch, gram_t.T


def solution(mesh):
    nrow = mesh.shape["row"]
    nz = mesh.shape["col"] // QUAD
    return jax.shard_map(
        functools.partial(per_device, nrow, nz),
        mesh=mesh,
        in_specs=(P("row", "col", None), P("row", "col"), P("col"), P()),
        out_specs=(P("row", "col"), P("row", "col")),
        check_vma=False,
    )
```

profile of v0, /device:TPU:7, one launch (start us, length us, event | category | flops | bytes accessed | tf_op | source)
XLA Modules:
  0.0 48.2 jit_solution(9238849688764247301)
XLA Ops:
  0.6 46.3 %shard_map.59 = (f32[64,64]{1,0:T(8,128)S(1)}, f32[64,512]{1,0:T(8,128)S(1)}) custom-call(bf16[6,64,512]{2,1,0:T(8,128)(2,1)} %bitcast.5, s32[1,6]{1,0:T(1,128)} %block_hbm.1, s32[32,128]{1,0:T(8,128)} %bitcast.6, s32[32,128]{1,0:T(8,128)} %bitcast.7), custom_call_target="tpu_custom_call" | custom-call | tf_op jit(solution)/shard_map/pallas_call | solution.py:329
  47.0 0.6 %copy.8 = f32[64,64]{1,0:T(8,128)} copy(f32[64,64]{1,0:T(8,128)S(1)} %get-tuple-element.8) | data formatting | bytes 32768
  47.6 0.7 %copy.9 = f32[512,64]{0,1:T(8,128)} copy(f32[512,64]{0,1:T(8,128)S(1)} %bitcast.4) | data formatting | bytes 262144
where the time goes:
time: 48.5 us; the launch traced here: 48.2 us
  Pallas kernels  46.3 us (95%)
  local copies, waits for them, and re-layouts  1.27 us (3%)
  between operations  0.64 us (1%)
    pallas_call x1, Pallas kernels, per_device(): pl.pallas_call(functools.partial(kernel, nrow, nz), out_shape=(jax.ShapeD...  46.3 us
    unnamed x2, local copies, waits for them, and re-layouts  1.27 us

commit v1 on v0

--- a/solution.py
+++ b/solution.py
@@ -13,6 +13,8 @@
 CORES = 2
 QUAD = CHIPS * CORES
 LANES = 128
+XNEAR = 4
+ZNEAR = 1
 F32 = jnp.float32
 BF16 = jnp.bfloat16
 
@@ -56,15 +58,20 @@
     signs,
     samples,
     xs,
-    hop,
+    hop0,
+    hop1,
     terms,
     terms2,
     halves,
     other,
     other2,
+    far,
+    far2,
     own,
     csend,
     crecv,
+    nsend,
+    nrecv,
     ag,
     sk,
     sc,
@@ -75,9 +82,12 @@
     a_send,
     a_recv,
     x_send,
+    y_send,
     x_recv,
     c_send,
     c_recv,
+    n_send,
+    n_recv,
     g_send,
     g_recv,
     k_send,
@@ -150,33 +160,31 @@
             cut = slice(j * LANES, (j + 1) * LANES)
             xs[t * rows : (t + 1) * rows, cut] = tl[t, :, cut] * sign
 
-    low_bits = (tile_width - 1).bit_length()
-    fetches[3].wait()
-
-    def fill(blk, _):
-        low = samples[pl.ds(blk, 1), :] & (tile_width - 1)
-        lanes = pl.ds(pl.multiple_of(blk * LANES, LANES), LANES)
-        base = parity_sign(lax.broadcasted_iota(jnp.int32, (16, LANES), 0) & low).astype(BF16)
-        group = [base]
-        for bit in range(4, low_bits):
-            sign = (1 - 2 * ((low >> bit) & 1)).astype(F32)
-            sign = jnp.broadcast_to(sign, (16, LANES)).astype(BF16)
-            group = group + [g * sign for g in group]
-        for i, g in enumerate(group):
-            hop[16 * i : 16 * i + 16, lanes] = g
-        return 0
-
-    lax.fori_loop(0, width // LANES, fill, 0)
-
     def chunk_of(k):
         return lax.rem(my_chunk + nchunk // 2 + alternating(k) + nchunk, nchunk)
 
-    def multiply(k, _):
+    low_bits = (tile_width - 1).bit_length()
+    blocks_of_chunk = chunk // LANES
+    fetches[3].wait()
+
+    def build(k, hop):
         ch = chunk_of(k)
-        operator = hop[:, pl.ds(pl.multiple_of(ch * chunk, chunk), chunk)]
-        y = jnp.dot(xs[...], operator, preferred_element_type=F32)
-        for i in range(chunk // LANES):
-            high = samples[pl.ds(ch * (chunk // LANES) + i, 1), :] >> low_bits
+        for i in range(blocks_of_chunk):
+            low = samples[pl.ds(ch * blocks_of_chunk + i, 1), :] & (tile_width - 1)
+            base = parity_sign(lax.broadcasted_iota(jnp.int32, (16, LANES), 0) & low).astype(BF16)
+            group = [base]
+            for bit in range(4, low_bits):
+                sign = (1 - 2 * ((low >> bit) & 1)).astype(F32)
+                sign = jnp.broadcast_to(sign, (16, LANES)).astype(BF16)
+                group = group + [g * sign for g in group]
+            for j, g in enumerate(group):
+                hop[16 * j : 16 * j + 16, i * LANES : (i + 1) * LANES] = g
+
+    def multiply(k, hop):
+        ch = chunk_of(k)
+        y = jnp.dot(xs[...], hop[...], preferred_element_type=F32)
+        for i in range(blocks_of_chunk):
+            high = samples[pl.ds(ch * blocks_of_chunk + i, 1), :] >> low_bits
             coef = parity_sign(codes & high)
             total = None
             for t in range(slots):
@@ -184,55 +192,82 @@
                 total = term if total is None else total + term
             for p in range(CORES):
                 terms[k, p, :, i * LANES : (i + 1) * LANES] = total[p * part : (p + 1) * part]
-        return 0
-
-    lax.fori_loop(0, nchunk, multiply, 0)
-
-    pl.semaphore_wait(barrier, nz - 1 + nrow * QUAD - 1)
-
-    def to_sibling(k, _):
+
+    def to_sibling(k):
         remote(terms.at[k, 1 - core], terms2.at[k], a_send, a_recv.at[k], sibling).start()
-        return 0
-
-    lax.fori_loop(0, nchunk, to_sibling, 0)
-
-    def to_partner(k, _):
+
+    xfar = nchunk - XNEAR
+    zfar = nchunk - ZNEAR
+
+    def to_partner(k):
         wait_bytes(terms2.at[k], a_recv.at[k])
         total = terms[k, core] + terms2[k]
         for i in range(planes):
             left = total[:, 2 * i * LANES : (2 * i + 1) * LANES]
             right = total[:, (2 * i + 1) * LANES : (2 * i + 2) * LANES]
             halves[k, i] = jnp.where(h == 0, left, right)
-            other[k, i] = jnp.where(h == 0, right, left)
-        remote(other.at[k], other2.at[k], x_send, x_recv.at[k], partner).start()
-        return 0
-
-    lax.fori_loop(0, nchunk, to_partner, 0)
-
-    def to_planes(k, _):
-        wait_bytes(other2.at[k], x_recv.at[k])
+            given = jnp.where(h == 0, right, left)
+            if k < xfar:
+                far[k, i] = given.astype(BF16)
+            else:
+                other[k - xfar, i] = given
+        if k < xfar:
+            remote(far.at[k], far2.at[k], x_send, x_recv.at[k], partner).start()
+        else:
+            remote(other.at[k - xfar], other2.at[k - xfar], y_send, x_recv.at[k], partner).start()
+
+    build(0, hop0)
+
+    def pair(j, _):
+        k = 2 * j
+        build(k + 1, hop1)
+        multiply(k, hop0)
+        build(lax.rem(k + 2, nchunk), hop0)
+        multiply(k + 1, hop1)
+        return 0
+
+    lax.fori_loop(0, nchunk // 2, pair, 0)
+
+    pl.semaphore_wait(barrier, nz - 1 + nrow * QUAD - 1)
+    for k in range(nchunk):
+        to_sibling(k)
+    for k in range(nchunk):
+        to_partner(k)
+
+    side = lax.rem(z, planes)
+    for k in range(nchunk):
+        arrived = far2.at[k] if k < xfar else other2.at[k - xfar]
+        wait_bytes(arrived, x_recv.at[k])
         for i in range(planes):
-            z2 = chunk_of(k) * planes + i
-            total = halves[k, i] + other2[k, i]
-
-            @pl.when(z2 == z)
-            def _():
-                own[...] = total
-
-            @pl.when(z2 != z)
-            def _():
-                csend[z2] = total.astype(BF16)
-                slot = lax.rem(z - z2 + nz, nz) - 1
-                remote(csend.at[z2], crecv.at[slot], c_send, c_recv, (row, at(z2, h, core))).start()
-
-        return 0
-
-    lax.fori_loop(0, nchunk, to_planes, 0)
-
+            total = halves[k, i] + arrived[i].astype(F32)
+            device = (row, at(chunk_of(k) * planes + i, h, core))
+            if k < zfar:
+                csend[k, i] = total.astype(BF16)
+                remote(csend.at[k, i], crecv.at[k, side], c_send, c_recv, device).start()
+            elif k < nchunk - 1:
+                nsend[k - zfar, i] = total
+                slot = (k - zfar) * planes + side
+                remote(nsend.at[k - zfar, i], nrecv.at[slot], n_send, n_recv, device).start()
+            else:
+
+                @pl.when(side == i)
+                def _():
+                    own[...] = total
+
+                @pl.when(side != i)
+                def _():
+                    nsend[k - zfar, i] = total
+                    slot = (ZNEAR - 1) * planes + lax.rem(side - i + planes, planes) - 1
+                    remote(nsend.at[k - zfar, i], nrecv.at[slot], n_send, n_recv, device).start()
+
+    wait_bytes(nrecv, n_recv)
+    total = own[...]
+    for i in range(ZNEAR * planes - 1):
+        total = total + nrecv[i]
     wait_bytes(crecv, c_recv)
-    total = own[...]
-    for i in range(nz - 1):
-        total = total + crecv[i].astype(F32)
+    for k in range(zfar):
+        for i in range(planes):
+            total = total + crecv[k, i].astype(F32)
     total = total * (1.0 / math.sqrt(width))
     ag[z] = total.astype(BF16)
 
@@ -308,11 +343,24 @@
     gram_ref[:, cols:] = jnp.where(core == 0, theirs, mine)
 
     wait_bytes(terms2, a_send)
-    wait_bytes(other2, x_send)
+    wait_bytes(far2, x_send)
+    wait_bytes(other2, y_send)
     wait_bytes(crecv, c_send)
-    wait_bytes(crecv, g_send)
+    wait_bytes(nrecv, n_send)
+    wait_bytes(ag.at[pl.ds(0, nz - 1)], g_send)
     wait_bytes(sc.at[pl.ds(0, rows * nrow - part)], s_send)
     wait_bytes(sr.at[pl.ds(0, rows * nrow - part // CHIPS)], f_send)
+
+
+def store(sketch_ref, gram_ref, sketch_hbm, gram_hbm, sems):
+    copies = [
+        pltpu.make_async_copy(src, dst, sems.at[i])
+        for i, (src, dst) in enumerate([(gram_ref, gram_hbm), (sketch_ref, sketch_hbm)])
+    ]
+    for copy in copies:
+        copy.start()
+    for copy in copies:
+        copy.wait()
 
 
 def per_device(nrow, nz, tiles, block_cols, signs, samples):
@@ -340,15 +388,20 @@
             pltpu.VMEM((signs.shape[0] // LANES, LANES), jnp.int32),
             pltpu.VMEM((width // LANES, LANES), jnp.int32),
             pltpu.VMEM((slots * rows, tile_width), BF16),
-            pltpu.VMEM((tile_width, width), BF16),
+            pltpu.VMEM((tile_width, chunk), BF16),
+            pltpu.VMEM((tile_width, chunk), BF16),
             pltpu.VMEM((nchunk, CORES, part, chunk), F32),
             pltpu.VMEM((nchunk, part, chunk), F32),
             pltpu.VMEM((nchunk, planes, part, LANES), F32),
-            pltpu.VMEM((nchunk, planes, part, LANES), F32),
-            pltpu.VMEM((nchunk, planes, part, LANES), F32),
+            pltpu.VMEM((XNEAR, planes, part, LANES), F32),
+            pltpu.VMEM((XNEAR, planes, part, LANES), F32),
+            pltpu.VMEM((nchunk - XNEAR, planes, part, LANES), BF16),
+            pltpu.VMEM((nchunk - XNEAR, planes, part, LANES), BF16),
             pltpu.VMEM((part, LANES), F32),
-            pltpu.VMEM((nz, part, LANES), BF16),
-            pltpu.VMEM((nz - 1, part, LANES), BF16),
+            pltpu.VMEM((nchunk - ZNEAR, planes, part, LANES), BF16),
+            pltpu.VMEM((nchunk - ZNEAR, planes, part, LANES), BF16),
+            pltpu.VMEM((ZNEAR, planes, part, LANES), F32),
+            pltpu.VMEM((ZNEAR * planes - 1, part, LANES), F32),
             pltpu.VMEM((nz, part, LANES), BF16),
             pltpu.VMEM((2, part, LANES), F32),
             pltpu.VMEM((rows * nrow, LANES), BF16),
@@ -359,7 +412,10 @@
             dma,
             dma((nchunk,)),
             dma,
+            dma,
             dma((nchunk,)),
+            dma,
+            dma,
             dma,
             dma,
             dma,
@@ -387,6 +443,19 @@
             )
         )
     )
+    sketch, gram_t = pl.pallas_call(
+        store,
+        out_shape=(
+            jax.ShapeDtypeStruct(sketch.shape, F32),
+            jax.ShapeDtypeStruct(gram_t.shape, F32),
+        ),
+        in_specs=[vmem, vmem],
+        out_specs=(hbm, hbm),
+        scratch_shapes=[dma((2,))],
+    )(
+        pltpu.with_memory_space_constraint(sketch, pltpu.VMEM),
+        pltpu.with_memory_space_constraint(gram_t, pltpu.VMEM),
+    )
     return sketch, gram_t.T
 
 

time: 48.5 us -> 46.6 us (0.961)
  local copies, waits for them, and re-layouts: 1.27 us -> 0 us
  Pallas kernels: 46.3 us -> 45.8 us
    unnamed x2 -> x0, local copies, waits for them, and re-layouts: 1.27 us -> none
    pallas_call x1, Pallas kernels: 46.3 us -> 45.1 us  [per_device(): pl.pallas_call(functools.partial(kernel, nrow, nz), out_shape=(jax.ShapeD...]
    pallas_call x0 -> x1, Pallas kernels: none -> 0.68 us  [per_device(): pl.pallas_call(store, out_shape=(jax.ShapeDtypeStruct(sketch.shape, F32),...]
where the time goes in v1:
time: 46.6 us; the launch traced here: 46.5 us
  Pallas kernels  45.8 us (98%)
  between operations  0.64 us (1%)
    pallas_call x1, Pallas kernels, per_device(): pl.pallas_call(functools.partial(kernel, nrow, nz), out_shape=(jax.ShapeD...  45.1 us

profile of v1, /device:TPU:7, one launch (start us, length us, event | category | flops | bytes accessed | tf_op | source)
XLA Modules:
  0.0 46.5 jit_solution(4022307795080671592)
XLA Ops:
  0.6 45.1 %shard_map.59 = (f32[64,64]{1,0:T(8,128)S(1)}, f32[64,512]{1,0:T(8,128)S(1)}) custom-call(bf16[6,64,512]{2,1,0:T(8,128)(2,1)} %bitcast.4, s32[1,6]{1,0:T(1,128)} %block_hbm.1, s32[32,128]{1,0:T(8,128)} %bitcast.5, s32[32,128]{1,0:T(8,128)} %bitcast.6), custom_call_target="tpu_custom_call" | custom-call | tf_op jit(solution)/shard_map/pallas_call | solution.py:377
  45.8 0.7 %shard_map.60 = (f32[64,64]{1,0:T(8,128)}, f32[64,512]{1,0:T(8,128)}) custom-call(f32[64,64]{1,0:T(8,128)S(1)} %get-tuple-element.6.sketch_ref, f32[64,512]{1,0:T(8,128)S(1)} %get-tuple-element.7.gram_ref), custom_call_target="tpu_custom_call" | custom-call | tf_op jit(solution)/shard_map/pallas_call | solution.py:446

commit v2 on v1

--- a/solution.py
+++ b/solution.py
@@ -13,7 +13,7 @@
 CORES = 2
 QUAD = CHIPS * CORES
 LANES = 128
-XNEAR = 4
+XNEAR = 5
 ZNEAR = 1
 F32 = jnp.float32
 BF16 = jnp.bfloat16
@@ -94,6 +94,8 @@
     k_recv,
     s_send,
     s_recv,
+    w_send,
+    w_recv,
     f_send,
     f_recv,
     o_send,
@@ -281,13 +283,12 @@
     my_rows = pl.ds(pl.multiple_of(row * rows + core * part, part), part)
 
     def in_plane(k, _):
-        mate = lax.rem(row * CORES + core + k, nrow * CORES)
-        device = (lax.div(mate, CORES), at(z, h, lax.rem(mate, CORES)))
-        remote(ag.at[z], sc.at[my_rows], s_send, s_recv, device).start()
-        return 0
-
-    lax.fori_loop(1, nrow * CORES, in_plane, 0)
-    pltpu.make_async_copy(ag.at[z], sc.at[my_rows], s_recv).start()
+        device = (lax.rem(row + k, nrow), col)
+        remote(ag.at[z], sc.at[row, core], s_send, s_recv, device).start()
+        return 0
+
+    lax.fori_loop(1, nrow, in_plane, 0)
+    pltpu.make_async_copy(ag.at[z], sc.at[row, core], s_recv).start()
 
     sk[0] = total
     swap_sketch = remote(sk.at[0], sk.at[1], k_send, k_recv, sibling)
@@ -321,16 +322,20 @@
 
     lax.fori_loop(0, nrow, forward, 0)
 
+    wait_bytes(sc.at[:, core], s_recv)
+    swap_columns = remote(sc.at[:, core], sc.at[:, core], w_send, w_recv, sibling)
+    swap_columns.start()
+
     half = LANES // CORES
     swap_sketch.wait()
     for i in range(CORES):
         block = sk[jnp.where(core == i, 0, 1)]
         sketch_ref[i * part : (i + 1) * part, :] = jnp.where(core == 0, block[:, :half], block[:, half:])
 
-    wait_bytes(sc, s_recv)
+    swap_columns.wait()
     wait_bytes(sr, f_recv)
     product = lax.dot_general(
-        sc[...], sr[...], (((0,), (0,)), ((), ())), preferred_element_type=F32
+        sc[...].reshape(rows * nrow, LANES), sr[...], (((0,), (0,)), ((), ())), preferred_element_type=F32
     ) * (1.0 / (rows * nrow))
     gs[...] = jnp.where(core == 0, product[half:], product[:half])
     swap_product = remote(gs, gr, o_send, o_recv, sibling)
@@ -348,7 +353,7 @@
     wait_bytes(crecv, c_send)
     wait_bytes(nrecv, n_send)
     wait_bytes(ag.at[pl.ds(0, nz - 1)], g_send)
-    wait_bytes(sc.at[pl.ds(0, rows * nrow - part)], s_send)
+    wait_bytes(sc.at[pl.ds(0, nrow - 1), 0], s_send)
     wait_bytes(sr.at[pl.ds(0, rows * nrow - part // CHIPS)], f_send)
 
 
@@ -404,7 +409,7 @@
             pltpu.VMEM((ZNEAR * planes - 1, part, LANES), F32),
             pltpu.VMEM((nz, part, LANES), BF16),
             pltpu.VMEM((2, part, LANES), F32),
-            pltpu.VMEM((rows * nrow, LANES), BF16),
+            pltpu.VMEM((nrow, CORES, part, LANES), BF16),
             pltpu.VMEM((rows * nrow, CHIPS * LANES), BF16),
             pltpu.VMEM((half, CHIPS * LANES), F32),
             pltpu.VMEM((half, CHIPS * LANES), F32),
@@ -420,6 +425,8 @@
             dma,
             dma,
             dma((nz,)),
+            dma,
+            dma,
             dma,
             dma,
             dma,

time: 46.6 us -> 46.6 us (level)
  no operation moved by 1% of the time
where the time goes in v2:
time: 46.6 us; the launch traced here: 46.4 us
  Pallas kernels  45.8 us (98%)
  between operations  0.64 us (1%)
    pallas_call x1, Pallas kernels, per_device(): pl.pallas_call(functools.partial(kernel, nrow, nz), out_shape=(jax.ShapeD...  45.1 us

profile of v2, /device:TPU:7, one launch (start us, length us, event | category | flops | bytes accessed | tf_op | source)
XLA Modules:
  0.0 46.4 jit_solution(13474966785212913707)
XLA Ops:
  0.6 45.1 %shard_map.59 = (f32[64,64]{1,0:T(8,128)S(1)}, f32[64,512]{1,0:T(8,128)S(1)}) custom-call(bf16[6,64,512]{2,1,0:T(8,128)(2,1)} %bitcast.4, s32[1,6]{1,0:T(1,128)} %block_hbm.1, s32[32,128]{1,0:T(8,128)} %bitcast.5, s32[32,128]{1,0:T(8,128)} %bitcast.6), custom_call_target="tpu_custom_call" | custom-call | tf_op jit(solution)/shard_map/pallas_call | solution.py:382
  45.8 0.7 %shard_map.60 = (f32[64,64]{1,0:T(8,128)}, f32[64,512]{1,0:T(8,128)}) custom-call(f32[64,64]{1,0:T(8,128)S(1)} %get-tuple-element.6.sketch_ref, f32[64,512]{1,0:T(8,128)S(1)} %get-tuple-element.7.gram_ref), custom_call_target="tpu_custom_call" | custom-call | tf_op jit(solution)/shard_map/pallas_call | solution.py:453

commit v3 on v2

--- a/solution.py
+++ b/solution.py
@@ -295,32 +295,24 @@
     swap_sketch.start()
 
     my_cols = pl.ds(pl.multiple_of(h * LANES, LANES), LANES)
-
-    def forward(k, _):
-        p = lax.rem(my_chunk + alternating(k) + nrow, nrow)
-        for i in range(planes):
-            z2 = p * planes + i
-
-            @pl.when(z2 != z)
+    for k in range(nz):
+        offset = (k + 1) // 2 * (1 if k % 2 else -1)
+        z2 = lax.rem(z - offset + nz, nz)
+        if offset:
+            wait_bytes(ag.at[z2], g_recv.at[z2])
+        p = lax.div(z2, planes)
+        i = lax.rem(z2, planes)
+        for h2 in range(CHIPS):
+            here = jnp.logical_and(p == row, jnp.logical_and(h2 == h, i == core))
+
+            @pl.when(here)
             def _():
-                wait_bytes(ag.at[z2], g_recv.at[z2])
-
-            for h2 in range(CHIPS):
-                here = jnp.logical_and(p == row, jnp.logical_and(h2 == h, i == core))
-
-                @pl.when(here)
-                def _():
-                    pltpu.make_async_copy(ag.at[z2], sr.at[my_rows, my_cols], f_recv).start()
-
-                @pl.when(jnp.logical_not(here))
-                def _():
-                    remote(
-                        ag.at[z2], sr.at[my_rows, my_cols], f_send, f_recv, (p, at(z, h2, i))
-                    ).start()
-
-        return 0
-
-    lax.fori_loop(0, nrow, forward, 0)
+                pltpu.make_async_copy(ag.at[z2], sr.at[my_rows, my_cols], f_recv).start()
+
+            @pl.when(jnp.logical_not(here))
+            def _():
+                device = (p, at(z, h2, i))
+                remote(ag.at[z2], sr.at[my_rows, my_cols], f_send, f_recv, device).start()
 
     wait_bytes(sc.at[:, core], s_recv)
     swap_columns = remote(sc.at[:, core], sc.at[:, core], w_send, w_recv, sibling)

time: 46.6 us -> 46.7 us (level)
  no operation moved by 1% of the time
where the time goes in v3:
time: 46.7 us; the launch traced here: 46.6 us
  Pallas kernels  45.9 us (98%)
  between operations  0.64 us (1%)
    pallas_call x1, Pallas kernels, per_device(): pl.pallas_call(functools.partial(kernel, nrow, nz), out_shape=(jax.ShapeD...  45.2 us

profile of v3, /device:TPU:7, one launch (start us, length us, event | category | flops | bytes accessed | tf_op | source)
XLA Modules:
  0.0 46.6 jit_solution(3656905532122026510)
XLA Ops:
  0.6 45.2 %shard_map.59 = (f32[64,64]{1,0:T(8,128)S(1)}, f32[64,512]{1,0:T(8,128)S(1)}) custom-call(bf16[6,64,512]{2,1,0:T(8,128)(2,1)} %bitcast.4, s32[1,6]{1,0:T(1,128)} %block_hbm.1, s32[32,128]{1,0:T(8,128)} %bitcast.5, s32[32,128]{1,0:T(8,128)} %bitcast.6), custom_call_target="tpu_custom_call" | custom-call | tf_op jit(solution)/shard_map/pallas_call | solution.py:374
  45.9 0.7 %shard_map.60 = (f32[64,64]{1,0:T(8,128)}, f32[64,512]{1,0:T(8,128)}) custom-call(f32[64,64]{1,0:T(8,128)S(1)} %get-tuple-element.6.sketch_ref, f32[64,512]{1,0:T(8,128)S(1)} %get-tuple-element.7.gram_ref), custom_call_target="tpu_custom_call" | custom-call | tf_op jit(solution)/shard_map/pallas_call | solution.py:445

commit v4 on v2

--- a/solution.py
+++ b/solution.py
@@ -334,13 +334,18 @@
 
     swap_columns.wait()
     wait_bytes(sr, f_recv)
-    product = lax.dot_general(
-        sc[...].reshape(rows * nrow, LANES), sr[...], (((0,), (0,)), ((), ())), preferred_element_type=F32
-    ) * (1.0 / (rows * nrow))
-    gs[...] = jnp.where(core == 0, product[half:], product[:half])
+    columns = sc[...].reshape(rows * nrow, LANES)
+    low, high = columns[:, :half], columns[:, half:]
+
+    def product(left):
+        return lax.dot_general(
+            left, sr[...], (((0,), (0,)), ((), ())), preferred_element_type=F32
+        ) * (1.0 / (rows * nrow))
+
+    gs[...] = product(jnp.where(core == 0, high, low))
     swap_product = remote(gs, gr, o_send, o_recv, sibling)
     swap_product.start()
-    mine = jnp.where(core == 0, product[:half], product[half:])
+    mine = product(jnp.where(core == 0, low, high))
     swap_product.wait()
     theirs = gr[...]
     cols = CHIPS * LANES

time: 46.6 us -> 46.7 us (level)
  no operation moved by 1% of the time
where the time goes in v4:
time: 46.7 us; the launch traced here: 46.6 us
  Pallas kernels  46 us (99%)
  between operations  0.64 us (1%)
    pallas_call x1, Pallas kernels, per_device(): pl.pallas_call(functools.partial(kernel, nrow, nz), out_shape=(jax.ShapeD...  45.3 us

profile of v4, /device:TPU:7, one launch (start us, length us, event | category | flops | bytes accessed | tf_op | source)
XLA Modules:
  0.0 46.6 jit_solution(6890806270815428483)
XLA Ops:
  0.6 45.3 %shard_map.59 = (f32[64,64]{1,0:T(8,128)S(1)}, f32[64,512]{1,0:T(8,128)S(1)}) custom-call(bf16[6,64,512]{2,1,0:T(8,128)(2,1)} %bitcast.4, s32[1,6]{1,0:T(1,128)} %block_hbm.1, s32[32,128]{1,0:T(8,128)} %bitcast.5, s32[32,128]{1,0:T(8,128)} %bitcast.6), custom_call_target="tpu_custom_call" | custom-call | tf_op jit(solution)/shard_map/pallas_call | solution.py:387
  45.9 0.7 %shard_map.60 = (f32[64,64]{1,0:T(8,128)}, f32[64,512]{1,0:T(8,128)}) custom-call(f32[64,64]{1,0:T(8,128)S(1)} %get-tuple-element.6.sketch_ref, f32[64,512]{1,0:T(8,128)S(1)} %get-tuple-element.7.gram_ref), custom_call_target="tpu_custom_call" | custom-call | tf_op jit(solution)/shard_map/pallas_call | solution.py:458

commit v5 on v2

--- a/solution.py
+++ b/solution.py
@@ -294,29 +294,28 @@
     swap_sketch = remote(sk.at[0], sk.at[1], k_send, k_recv, sibling)
     swap_sketch.start()
 
-    my_cols = pl.ds(pl.multiple_of(h * LANES, LANES), LANES)
-
     def forward(k, _):
         p = lax.rem(my_chunk + alternating(k) + nrow, nrow)
+        first = p * planes
         for i in range(planes):
-            z2 = p * planes + i
+            z2 = first + i
 
             @pl.when(z2 != z)
             def _():
                 wait_bytes(ag.at[z2], g_recv.at[z2])
 
-            for h2 in range(CHIPS):
-                here = jnp.logical_and(p == row, jnp.logical_and(h2 == h, i == core))
-
-                @pl.when(here)
-                def _():
-                    pltpu.make_async_copy(ag.at[z2], sr.at[my_rows, my_cols], f_recv).start()
-
-                @pl.when(jnp.logical_not(here))
-                def _():
-                    remote(
-                        ag.at[z2], sr.at[my_rows, my_cols], f_send, f_recv, (p, at(z, h2, i))
-                    ).start()
+        src = ag.at[pl.ds(first, planes)]
+        dst = sr.at[:, my_rows]
+        for h2 in range(CHIPS):
+            here = jnp.logical_and(p == row, jnp.logical_and(h2 == h, core == h))
+
+            @pl.when(here)
+            def _():
+                pltpu.make_async_copy(src, dst, f_recv).start()
+
+            @pl.when(jnp.logical_not(here))
+            def _():
+                remote(src, dst, f_send, f_recv, (p, at(z, h2, h))).start()
 
         return 0
 
@@ -334,8 +333,13 @@
 
     swap_columns.wait()
     wait_bytes(sr, f_recv)
-    product = lax.dot_general(
-        sc[...].reshape(rows * nrow, LANES), sr[...], (((0,), (0,)), ((), ())), preferred_element_type=F32
+    columns = sc[...].reshape(rows * nrow, LANES)
+    product = jnp.concatenate(
+        [
+            lax.dot_general(columns, sr[i], (((0,), (0,)), ((), ())), preferred_element_type=F32)
+            for i in range(planes)
+        ],
+        axis=1,
     ) * (1.0 / (rows * nrow))
     gs[...] = jnp.where(core == 0, product[half:], product[:half])
     swap_product = remote(gs, gr, o_send, o_recv, sibling)
@@ -343,9 +347,11 @@
     mine = jnp.where(core == 0, product[:half], product[half:])
     swap_product.wait()
     theirs = gr[...]
-    cols = CHIPS * LANES
-    gram_ref[:, :cols] = jnp.where(core == 0, mine, theirs)
-    gram_ref[:, cols:] = jnp.where(core == 0, theirs, mine)
+    for i in range(planes):
+        cut = slice(i * LANES, (i + 1) * LANES)
+        left = 2 * i * LANES
+        gram_ref[:, left : left + LANES] = jnp.where(core == 0, mine[:, cut], theirs[:, cut])
+        gram_ref[:, left + LANES : left + 2 * LANES] = jnp.where(core == 0, theirs[:, cut], mine[:, cut])
 
     wait_bytes(terms2, a_send)
     wait_bytes(far2, x_send)
@@ -354,7 +360,14 @@
     wait_bytes(nrecv, n_send)
     wait_bytes(ag.at[pl.ds(0, nz - 1)], g_send)
     wait_bytes(sc.at[pl.ds(0, nrow - 1), 0], s_send)
-    wait_bytes(sr.at[pl.ds(0, rows * nrow - part // CHIPS)], f_send)
+
+    @pl.when(core == h)
+    def _():
+        wait_bytes(sr.at[:, pl.ds(0, rows * nrow - part)], f_send)
+
+    @pl.when(core != h)
+    def _():
+        wait_bytes(sr, f_send)
 
 
 def store(sketch_ref, gram_ref, sketch_hbm, gram_hbm, sems):
@@ -410,9 +423,9 @@
             pltpu.VMEM((nz, part, LANES), BF16),
             pltpu.VMEM((2, part, LANES), F32),
             pltpu.VMEM((nrow, CORES, part, LANES), BF16),
-            pltpu.VMEM((rows * nrow, CHIPS * LANES), BF16),
-            pltpu.VMEM((half, CHIPS * LANES), F32),
-            pltpu.VMEM((half, CHIPS * LANES), F32),
+            pltpu.VMEM((planes, rows * nrow, LANES), BF16),
+            pltpu.VMEM((half, planes * LANES), F32),
+            pltpu.VMEM((half, planes * LANES), F32),
             dma((4,)),
             dma,
             dma((nchunk,)),

time: 46.6 us -> 46.9 us (level)
  no operation moved by 1% of the time
where the time goes in v5:
time: 46.9 us; the launch traced here: 46.7 us
  Pallas kernels  46.1 us (98%)
  between operations  0.64 us (1%)
    pallas_call x1, Pallas kernels, per_device(): pl.pallas_call(functools.partial(kernel, nrow, nz), out_shape=(jax.ShapeD...  45.4 us

profile of v5, /device:TPU:7, one launch (start us, length us, event | category | flops | bytes accessed | tf_op | source)
XLA Modules:
  0.0 46.7 jit_solution(4511565265156232713)
XLA Ops:
  0.6 45.4 %shard_map.59 = (f32[64,64]{1,0:T(8,128)S(1)}, f32[64,512]{1,0:T(8,128)S(1)}) custom-call(bf16[6,64,512]{2,1,0:T(8,128)(2,1)} %bitcast.4, s32[1,6]{1,0:T(1,128)} %block_hbm.1, s32[32,128]{1,0:T(8,128)} %bitcast.5, s32[32,128]{1,0:T(8,128)} %bitcast.6), custom_call_target="tpu_custom_call" | custom-call | tf_op jit(solution)/shard_map/pallas_call | solution.py:395
  46.0 0.7 %shard_map.60 = (f32[64,64]{1,0:T(8,128)}, f32[64,512]{1,0:T(8,128)}) custom-call(f32[64,64]{1,0:T(8,128)S(1)} %get-tuple-element.6.sketch_ref, f32[64,512]{1,0:T(8,128)S(1)} %get-tuple-element.7.gram_ref), custom_call_target="tpu_custom_call" | custom-call | tf_op jit(solution)/shard_map/pallas_call | solution.py:466
